TPU v7x, 256 devices: a whole 4x4x8 slice. The times are simulated.
256 devices in a mesh: ctx: 32 (over z, y), kv: 8 (over x, core).
Axes of the slice: x: 4, y: 4, z: 8, core: 2. Of those that a mesh axis runs over, the one named last changes fastest.
Arguments:
- queries: bfloat16 [8192, 8192], P('ctx', 'kv'), may hold values from -120 to 120
- keys: bfloat16 [8192, 1024], P('ctx', 'kv'), may hold values from -8 to 8
- values: bfloat16 [8192, 1024], P('ctx', 'kv'), may hold values from -6 to 6
- retrieval: int32 [64], P('kv'), may hold values from 0 to 1, as said below
Outputs:
- attention_out: bfloat16 [8192, 8192], P(('ctx', 'kv'))
Inputs may be any that keep to these rules, and one draw needn't show every extreme that they name: `retrieval`: exactly 12 of the 64 entries are 1, the rest 0.
All inputs are finite; a program needn't handle non-finite values.
Results may differ from a plain program's by a relative error of at most 0.0045.
Values may be sent and summed in bfloat16 or wider, within the bound.
A program may use at most 64 MiB of HBM per device.

v0:
```python
import jax
import jax.numpy as jnp
from jax import lax
from jax.sharding import PartitionSpec as P

HD = 128
SINK = 64
WINDOW = 4096


NEG = -1e30


def start_state(heads, count):
    return (
        jnp.full((heads, count), NEG, jnp.float32),
        jnp.zeros((heads, count), jnp.float32),
        jnp.zeros((heads, count, HD), jnp.float32),
    )


def attend(state, q_heads, tpos, k_piece, v_piece, flags):
    width = k_piece.shape[0]
    spos = lax.iota(jnp.int32, width)
    causal = spos[None, :] <= tpos[:, None]
    near = (spos[None, :] < SINK) | (tpos[:, None] - spos[None, :] < WINDOW)
    any_causal = jnp.any(causal)
    any_near = jnp.any(causal & near)

    def one_head(operands):
        peak, total, numer, q_head, flag = operands
        needed = jnp.where(flag == 1, any_causal, any_near)

        def compute(unused):
            scores = jnp.dot(q_head, k_piece.T, preferred_element_type=jnp.float32) * HD ** (-0.5)
            allowed = causal & ((flag == 1) | near)
            masked = jnp.where(allowed, scores, NEG)
            new_peak = jnp.maximum(peak, jnp.max(masked, axis=1))
            weights = jnp.where(allowed, jnp.exp(masked - new_peak[:, None]), 0.0)
            fade = jnp.exp(peak - new_peak)
            new_total = total * fade + jnp.sum(weights, axis=1)
            new_numer = numer * fade[:, None] + jnp.dot(
                weights.astype(jnp.bfloat16), v_piece, preferred_element_type=jnp.float32
            )
            return (new_peak, new_total, new_numer)

        def keep(unused):
            return (peak, total, numer)

        return lax.cond(needed, compute, keep, 0)

    peak, total, numer = state
    return lax.map(one_head, (peak, total, numer, q_heads, flags))


def finish(state):
    peak, total, numer = state
    result = numer / total[..., None]
    heads, count, size = result.shape
    return jnp.transpose(result, (1, 0, 2)).reshape(count, heads * size).astype(jnp.bfloat16)


def shards(queries, keys, values, retrieval):
    rows = queries.shape[0]
    heads = queries.shape[1] // HD
    q_local = queries.reshape(rows, heads, HD)
    place = lax.axis_index("ctx")
    q_heads = jnp.transpose(q_local, (1, 0, 2))
    q_pos = place * rows + lax.iota(jnp.int32, rows)
    state = attend(
        start_state(heads, rows),
        q_heads,
        q_pos,
        lax.all_gather(keys, "ctx", axis=0, tiled=True),
        lax.all_gather(values, "ctx", axis=0, tiled=True),
        retrieval,
    )
    attention = finish(state)
    return lax.all_to_all(attention, "kv", split_axis=0, concat_axis=1, tiled=True)


def solution(mesh):
    return jax.shard_map(
        shards,
        mesh=mesh,
        in_specs=(P("ctx", "kv"), P("ctx", "kv"), P("ctx", "kv"), P("kv")),
        out_specs=P(("ctx", "kv"), None),
        check_vma=False,
    )
```

profile of v0, /device:TPU:225, one launch (start us, length us, event | category | flops | bytes accessed | tf_op | source)
XLA Modules:
  0.0 433.4 jit_solution(16388907582660619834)
XLA Ops:
  9.6 3.4 fusion.26
  13.0 70.1 %all-gather.3.cloned.1.call-done = bf16[8192,128]{1,0:T(8,128)(2,1)} async-done(((bf16[256,128]{1,0:T(8,128)(2,1)}), bf16[8192,128]{1,0:T(8,128)(2,1)}) %all-gather.3.cloned.1.call-update) | async-done | bytes 2097168 | tf_op jit(solution)/shard_map/all_gather | solution.py:74
  83.1 77.8 %all-gather.5.cloned.1.call-done = bf16[8192,128]{1,0:T(8,128)(2,1)} async-done(((bf16[256,128]{1,0:T(8,128)(2,1)}), bf16[8192,128]{1,0:T(8,128)(2,1)}) %all-gather.5.cloned.1.call-update) | async-done | bytes 2097168 | tf_op jit(solution)/shard_map/all_gather | solution.py:75
  160.9 244.7 %while.14 = (s32[]{:T(128)}, f32[8,256]{1,0:T(8,128)S(1)}, f32[8,256,128]{2,1,0:T(8,128)}, s32[8]{0:T(128)S(1)}, pred[]{:T(512)}, /*index=5*/pred[]{:T(512)}, bf...) while((s32[]{:T(128)}, f32[8,256]{1,0:T(8,128)S(1)}, ...), condition=%wide.region_7.8_spmd.clone.clone, body=%wide.region_2.7_spmd.clone.clone.sunk | while | flops 1105265408 | bytes 105736056 | solution.py:53
  161.5 3.8 le.71
  165.3 4.2 le.70
  171.3 19.4 %conditional.4 = (f32[1,256]{1,0:T(1,128)S(1)}, f32[1,256,128]{2,1,0:T(8,128)S(1)}) conditional(s32[]{:T(128)} %convert_element_type.34, (f32[256]{0:T(256)S(1)}, f32[256,128]{1,0:T(8,128)S(1)}) %tuple.76, (s32[]{:T(128)}, pred[8192]{0:T(1024)(128)(4,1)S(1)}, s32[256,8192]{1,0:T(8,128)}, bf16[8,256,128]{2,1,0:T(8,128)(2,1)S(1)}, s32[]{:T(128)}, ...), branch_computations={%region_3.3_spmd, %region_4.6_spmd.clone} | conditional | flops 1105265408 | bytes 80039992 | solution.py:50
  171.9 12.5 %fusion.7 = pred[256,8192]{1,0:T(32,128)(4,1)S(1)} fusion(s32[256,8192]{1,0:T(8,128)} %get-tuple-element.269, s32[256,8192]{1,0:T(8,128)} %get-tuple-element.272, s32[256,8192]{1,0:T(8,128)} %get-tuple-element.272, s32[256,8192]{1,0:T(8,128)} %get-tuple-element.269, pred[8192]{0:T(1024)(128)(4,1)S(1)} %get-tuple-element.270, pred[]{:T(512)S(6)} %eq.10), kind=kLoop, calls=%fused_computation.8 | loop fusion | flops 12582912 | bytes 35659776 | tf_op jit(solution)/shard_map/while/body/eval_jaxpr/cond/branch_1_fun/and | solution.py:36
  188.6 2.2 fusion.17
  192.1 3.8 le.71
  195.9 4.2 le.70
  201.9 19.5 %conditional.4 = (f32[1,256]{1,0:T(1,128)S(1)}, f32[1,256,128]{2,1,0:T(8,128)S(1)}) conditional(s32[]{:T(128)} %convert_element_type.34, (f32[256]{0:T(256)S(1)}, f32[256,128]{1,0:T(8,128)S(1)}) %tuple.76, (s32[]{:T(128)}, pred[8192]{0:T(1024)(128)(4,1)S(1)}, s32[256,8192]{1,0:T(8,128)}, bf16[8,256,128]{2,1,0:T(8,128)(2,1)S(1)}, s32[]{:T(128)}, ...), branch_computations={%region_3.3_spmd, %region_4.6_spmd.clone} | conditional | flops 1105265408 | bytes 80039992 | solution.py:50
  202.5 12.5 %fusion.7 = pred[256,8192]{1,0:T(32,128)(4,1)S(1)} fusion(s32[256,8192]{1,0:T(8,128)} %get-tuple-element.269, s32[256,8192]{1,0:T(8,128)} %get-tuple-element.272, s32[256,8192]{1,0:T(8,128)} %get-tuple-element.272, s32[256,8192]{1,0:T(8,128)} %get-tuple-element.269, pred[8192]{0:T(1024)(128)(4,1)S(1)} %get-tuple-element.270, pred[]{:T(512)S(6)} %eq.10), kind=kLoop, calls=%fused_computation.8 | loop fusion | flops 12582912 | bytes 35659776 | tf_op jit(solution)/shard_map/while/body/eval_jaxpr/cond/branch_1_fun/and | solution.py:36
  215.0 2.1 fusion.29
  219.2 2.2 fusion.17
  222.7 3.8 le.71
  226.5 4.2 le.70
  232.5 19.4 %conditional.4 = (f32[1,256]{1,0:T(1,128)S(1)}, f32[1,256,128]{2,1,0:T(8,128)S(1)}) conditional(s32[]{:T(128)} %convert_element_type.34, (f32[256]{0:T(256)S(1)}, f32[256,128]{1,0:T(8,128)S(1)}) %tuple.76, (s32[]{:T(128)}, pred[8192]{0:T(1024)(128)(4,1)S(1)}, s32[256,8192]{1,0:T(8,128)}, bf16[8,256,128]{2,1,0:T(8,128)(2,1)S(1)}, s32[]{:T(128)}, ...), branch_computations={%region_3.3_spmd, %region_4.6_spmd.clone} | conditional | flops 1105265408 | bytes 80039992 | solution.py:50
  233.1 12.5 %fusion.7 = pred[256,8192]{1,0:T(32,128)(4,1)S(1)} fusion(s32[256,8192]{1,0:T(8,128)} %get-tuple-element.269, s32[256,8192]{1,0:T(8,128)} %get-tuple-element.272, s32[256,8192]{1,0:T(8,128)} %get-tuple-element.272, s32[256,8192]{1,0:T(8,128)} %get-tuple-element.269, pred[8192]{0:T(1024)(128)(4,1)S(1)} %get-tuple-element.270, pred[]{:T(512)S(6)} %eq.10), kind=kLoop, calls=%fused_computation.8 | loop fusion | flops 12582912 | bytes 35659776 | tf_op jit(solution)/shard_map/while/body/eval_jaxpr/cond/branch_1_fun/and | solution.py:36
  249.8 2.2 fusion.17
  253.2 3.8 le.71
  257.1 4.2 le.70
  263.1 19.4 %conditional.4 = (f32[1,256]{1,0:T(1,128)S(1)}, f32[1,256,128]{2,1,0:T(8,128)S(1)}) conditional(s32[]{:T(128)} %convert_element_type.34, (f32[256]{0:T(256)S(1)}, f32[256,128]{1,0:T(8,128)S(1)}) %tuple.76, (s32[]{:T(128)}, pred[8192]{0:T(1024)(128)(4,1)S(1)}, s32[256,8192]{1,0:T(8,128)}, bf16[8,256,128]{2,1,0:T(8,128)(2,1)S(1)}, s32[]{:T(128)}, ...), branch_computations={%region_3.3_spmd, %region_4.6_spmd.clone} | conditional | flops 1105265408 | bytes 80039992 | solution.py:50
  263.7 12.5 %fusion.7 = pred[256,8192]{1,0:T(32,128)(4,1)S(1)} fusion(s32[256,8192]{1,0:T(8,128)} %get-tuple-element.269, s32[256,8192]{1,0:T(8,128)} %get-tuple-element.272, s32[256,8192]{1,0:T(8,128)} %get-tuple-element.272, s32[256,8192]{1,0:T(8,128)} %get-tuple-element.269, pred[8192]{0:T(1024)(128)(4,1)S(1)} %get-tuple-element.270, pred[]{:T(512)S(6)} %eq.10), kind=kLoop, calls=%fused_computation.8 | loop fusion | flops 12582912 | bytes 35659776 | tf_op jit(solution)/shard_map/while/body/eval_jaxpr/cond/branch_1_fun/and | solution.py:36
  276.2 2.1 fusion.29
  280.4 2.1 fusion.17
  283.8 3.8 le.71
  287.7 4.2 le.70
  293.7 19.4 %conditional.4 = (f32[1,256]{1,0:T(1,128)S(1)}, f32[1,256,128]{2,1,0:T(8,128)S(1)}) conditional(s32[]{:T(128)} %convert_element_type.34, (f32[256]{0:T(256)S(1)}, f32[256,128]{1,0:T(8,128)S(1)}) %tuple.76, (s32[]{:T(128)}, pred[8192]{0:T(1024)(128)(4,1)S(1)}, s32[256,8192]{1,0:T(8,128)}, bf16[8,256,128]{2,1,0:T(8,128)(2,1)S(1)}, s32[]{:T(128)}, ...), branch_computations={%region_3.3_spmd, %region_4.6_spmd.clone} | conditional | flops 1105265408 | bytes 80039992 | solution.py:50
  294.3 12.5 %fusion.7 = pred[256,8192]{1,0:T(32,128)(4,1)S(1)} fusion(s32[256,8192]{1,0:T(8,128)} %get-tuple-element.269, s32[256,8192]{1,0:T(8,128)} %get-tuple-element.272, s32[256,8192]{1,0:T(8,128)} %get-tuple-element.272, s32[256,8192]{1,0:T(8,128)} %get-tuple-element.269, pred[8192]{0:T(1024)(128)(4,1)S(1)} %get-tuple-element.270, pred[]{:T(512)S(6)} %eq.10), kind=kLoop, calls=%fused_computation.8 | loop fusion | flops 12582912 | bytes 35659776 | tf_op jit(solution)/shard_map/while/body/eval_jaxpr/cond/branch_1_fun/and | solution.py:36
  306.8 2.1 fusion.29
  311.0 2.1 fusion.17
  314.4 3.8 le.71
  318.2 4.2 le.70
  324.3 19.4 %conditional.4 = (f32[1,256]{1,0:T(1,128)S(1)}, f32[1,256,128]{2,1,0:T(8,128)S(1)}) conditional(s32[]{:T(128)} %convert_element_type.34, (f32[256]{0:T(256)S(1)}, f32[256,128]{1,0:T(8,128)S(1)}) %tuple.76, (s32[]{:T(128)}, pred[8192]{0:T(1024)(128)(4,1)S(1)}, s32[256,8192]{1,0:T(8,128)}, bf16[8,256,128]{2,1,0:T(8,128)(2,1)S(1)}, s32[]{:T(128)}, ...), branch_computations={%region_3.3_spmd, %region_4.6_spmd.clone} | conditional | flops 1105265408 | bytes 80039992 | solution.py:50
  324.9 12.5 %fusion.7 = pred[256,8192]{1,0:T(32,128)(4,1)S(1)} fusion(s32[256,8192]{1,0:T(8,128)} %get-tuple-element.269, s32[256,8192]{1,0:T(8,128)} %get-tuple-element.272, s32[256,8192]{1,0:T(8,128)} %get-tuple-element.272, s32[256,8192]{1,0:T(8,128)} %get-tuple-element.269, pred[8192]{0:T(1024)(128)(4,1)S(1)} %get-tuple-element.270, pred[]{:T(512)S(6)} %eq.10), kind=kLoop, calls=%fused_computation.8 | loop fusion | flops 12582912 | bytes 35659776 | tf_op jit(solution)/shard_map/while/body/eval_jaxpr/cond/branch_1_fun/and | solution.py:36
  341.6 2.2 fusion.17
  345.0 3.8 le.71
  348.9 4.2 le.70
  354.9 19.4 %conditional.4 = (f32[1,256]{1,0:T(1,128)S(1)}, f32[1,256,128]{2,1,0:T(8,128)S(1)}) conditional(s32[]{:T(128)} %convert_element_type.34, (f32[256]{0:T(256)S(1)}, f32[256,128]{1,0:T(8,128)S(1)}) %tuple.76, (s32[]{:T(128)}, pred[8192]{0:T(1024)(128)(4,1)S(1)}, s32[256,8192]{1,0:T(8,128)}, bf16[8,256,128]{2,1,0:T(8,128)(2,1)S(1)}, s32[]{:T(128)}, ...), branch_computations={%region_3.3_spmd, %region_4.6_spmd.clone} | conditional | flops 1105265408 | bytes 80039992 | solution.py:50
  355.5 12.5 %fusion.7 = pred[256,8192]{1,0:T(32,128)(4,1)S(1)} fusion(s32[256,8192]{1,0:T(8,128)} %get-tuple-element.269, s32[256,8192]{1,0:T(8,128)} %get-tuple-element.272, s32[256,8192]{1,0:T(8,128)} %get-tuple-element.272, s32[256,8192]{1,0:T(8,128)} %get-tuple-element.269, pred[8192]{0:T(1024)(128)(4,1)S(1)} %get-tuple-element.270, pred[]{:T(512)S(6)} %eq.10), kind=kLoop, calls=%fused_computation.8 | loop fusion | flops 12582912 | bytes 35659776 | tf_op jit(solution)/shard_map/while/body/eval_jaxpr/cond/branch_1_fun/and | solution.py:36
  372.2 2.2 fusion.17
  375.6 3.8 le.71
  379.5 4.2 le.70
  385.5 19.4 %conditional.4 = (f32[1,256]{1,0:T(1,128)S(1)}, f32[1,256,128]{2,1,0:T(8,128)S(1)}) conditional(s32[]{:T(128)} %convert_element_type.34, (f32[256]{0:T(256)S(1)}, f32[256,128]{1,0:T(8,128)S(1)}) %tuple.76, (s32[]{:T(128)}, pred[8192]{0:T(1024)(128)(4,1)S(1)}, s32[256,8192]{1,0:T(8,128)}, bf16[8,256,128]{2,1,0:T(8,128)(2,1)S(1)}, s32[]{:T(128)}, ...), branch_computations={%region_3.3_spmd, %region_4.6_spmd.clone} | conditional | flops 1105265408 | bytes 80039992 | solution.py:50
  386.1 12.5 %fusion.7 = pred[256,8192]{1,0:T(32,128)(4,1)S(1)} fusion(s32[256,8192]{1,0:T(8,128)} %get-tuple-element.269, s32[256,8192]{1,0:T(8,128)} %get-tuple-element.272, s32[256,8192]{1,0:T(8,128)} %get-tuple-element.272, s32[256,8192]{1,0:T(8,128)} %get-tuple-element.269, pred[8192]{0:T(1024)(128)(4,1)S(1)} %get-tuple-element.270, pred[]{:T(512)S(6)} %eq.10), kind=kLoop, calls=%fused_computation.8 | loop fusion | flops 12582912 | bytes 35659776 | tf_op jit(solution)/shard_map/while/body/eval_jaxpr/cond/branch_1_fun/and | solution.py:36
  402.8 2.2 fusion.17
  407.8 17.9 %all_to_all.16 = bf16[8,32,1024]{2,1,0:T(8,128)(2,1)S(1)} all-to-all(bf16[8,32,1024]{2,1,0:T(8,128)(2,1)S(1)} %convert_element_type.20), channel_id=1, replica_groups=mesh['ctx'=32,'kv'=8] {'kv'}, dimensions={0} | all-to-all | bytes 1048576 | tf_op jit(solution)/shard_map/all_to_all | solution.py:79
  (133 shorter events, 43.6 us)
Async XLA Ops:
  6.5 154.4 %copy-start.2 = (s32[8]{0:T(128)S(1)}, s32[8]{0:T(128)}, u32[]{:S(2)}) copy-start(s32[8]{0:T(128)} %param.11) | copy-start | bytes 100
  6.5 76.6 %all-gather.3.cloned.1.call-start = ((), (), s32[]{:S(2)}) async-start(), calls=%async_computation.1 | async-start | bytes 2162688 | tf_op jit(solution)/shard_map/all_gather | solution.py:74
  7.3 153.6 %all-gather.5.cloned.1.call-start = ((), (), s32[]{:S(2)}) async-start(), calls=%async_computation.2 | async-start | bytes 2162688 | tf_op jit(solution)/shard_map/all_gather | solution.py:75
  165.3 6.0 %copy-start = (bf16[8192,128]{1,0:T(8,128)(2,1)S(1)}, bf16[8192,128]{1,0:T(8,128)(2,1)}, u32[]{:S(2)}) copy-start(bf16[8192,128]{1,0:T(8,128)(2,1)} %get-tuple-element.437) | copy-start | bytes 6291460 | tf_op jit(solution)/shard_map/while
  186.5 2.1 copy-start.1
  195.9 6.0 %copy-start = (bf16[8192,128]{1,0:T(8,128)(2,1)S(1)}, bf16[8192,128]{1,0:T(8,128)(2,1)}, u32[]{:S(2)}) copy-start(bf16[8192,128]{1,0:T(8,128)(2,1)} %get-tuple-element.437) | copy-start | bytes 6291460 | tf_op jit(solution)/shard_map/while
  217.1 2.1 copy-start.1
  226.5 6.0 %copy-start = (bf16[8192,128]{1,0:T(8,128)(2,1)S(1)}, bf16[8192,128]{1,0:T(8,128)(2,1)}, u32[]{:S(2)}) copy-start(bf16[8192,128]{1,0:T(8,128)(2,1)} %get-tuple-element.437) | copy-start | bytes 6291460 | tf_op jit(solution)/shard_map/while
  247.7 2.1 copy-start.1
  257.1 6.0 %copy-start = (bf16[8192,128]{1,0:T(8,128)(2,1)S(1)}, bf16[8192,128]{1,0:T(8,128)(2,1)}, u32[]{:S(2)}) copy-start(bf16[8192,128]{1,0:T(8,128)(2,1)} %get-tuple-element.437) | copy-start | bytes 6291460 | tf_op jit(solution)/shard_map/while
  278.3 2.1 copy-start.1
  287.7 6.0 %copy-start = (bf16[8192,128]{1,0:T(8,128)(2,1)S(1)}, bf16[8192,128]{1,0:T(8,128)(2,1)}, u32[]{:S(2)}) copy-start(bf16[8192,128]{1,0:T(8,128)(2,1)} %get-tuple-element.437) | copy-start | bytes 6291460 | tf_op jit(solution)/shard_map/while
  308.9 2.1 copy-start.1
  318.2 6.0 %copy-start = (bf16[8192,128]{1,0:T(8,128)(2,1)S(1)}, bf16[8192,128]{1,0:T(8,128)(2,1)}, u32[]{:S(2)}) copy-start(bf16[8192,128]{1,0:T(8,128)(2,1)} %get-tuple-element.437) | copy-start | bytes 6291460 | tf_op jit(solution)/shard_map/while
  339.5 2.1 copy-start.1
  348.9 6.0 %copy-start = (bf16[8192,128]{1,0:T(8,128)(2,1)S(1)}, bf16[8192,128]{1,0:T(8,128)(2,1)}, u32[]{:S(2)}) copy-start(bf16[8192,128]{1,0:T(8,128)(2,1)} %get-tuple-element.437) | copy-start | bytes 6291460 | tf_op jit(solution)/shard_map/while
  370.1 2.1 copy-start.1
  379.5 6.0 %copy-start = (bf16[8192,128]{1,0:T(8,128)(2,1)S(1)}, bf16[8192,128]{1,0:T(8,128)(2,1)}, u32[]{:S(2)}) copy-start(bf16[8192,128]{1,0:T(8,128)(2,1)} %get-tuple-element.437) | copy-start | bytes 6291460 | tf_op jit(solution)/shard_map/while
  400.7 2.1 copy-start.1
Sparse Core Ops, SparseCore 0:
  9.9 73.1 all-gather.2
  85.7 75.1 all-gather.4
where the time goes:
time: 439 us; the launch traced here: 433 us
  waiting for transfers between devices  149 us (34%)
  other arithmetic  122 us (28%)
  local copies, waits for them, and re-layouts  77.4 us (18%)
  matrix products  34 us (8%)
  loops' own time  19.7 us (4%)
  blocking collectives  17.9 us (4%)
  between operations  13.5 us (3%)
    and x8, other arithmetic, compute(): allowed = causal & ((flag == 1) | near)  100 us
    all_gather x1, waiting for transfers between devices, shards(): lax.all_gather(values, 'ctx', axis=0, tiled=True)  77.8 us
    all_gather x1, waiting for transfers between devices, shards(): lax.all_gather(keys, 'ctx', axis=0, tiled=True)  70.1 us
    le x16, local copies, waits for them, and re-layouts, attend(): causal = spos[None, :] <= tpos[:, None]  63.9 us
    all_to_all x1, blocking collectives, shards(): lax.all_to_all(attention, 'kv', split_axis=0, concat_axis=1, tiled=True)  17.9 us
    dot_general x8, matrix products, compute(): jnp.dot(weights.astype(jnp.bfloat16), v_piece, preferred_element_type=jnp...  17.2 us
    dot_general x8, matrix products, compute(): jnp.dot(q_head, k_piece.T, preferred_element_type=jnp.float32)  16.8 us
    reduce_sum x8, other arithmetic, compute(): new_total = total * fade + jnp.sum(weights, axis=1)  16.5 us
  transfers between devices with their start and end apart: 2, of which 2 were waited for; matrix products, arithmetic and copies ran while one was open for 1% of the time, Pallas kernels for 0%

commit v1 on v0

v1 whole, which is shorter than its diff:
```python
import functools

import jax
import jax.numpy as jnp
from jax import lax
from jax.experimental import pallas as pl
from jax.experimental.pallas import tpu as pltpu
from jax.sharding import PartitionSpec as P

HD = 128
HQ = 8
SINK = 64
WINDOW = 4096
NEG = -1e30
SCALE = HD ** (-0.5) * 1.4426950408889634

NY = 4
NZ = 8
NKV = 8
BLOCK = 256
PLANE = NY * BLOCK
HALF = BLOCK // 2
GROUPS = 4
WIDE = HQ * HD // GROUPS
MESH = pl.DeviceIdType.MESH


def kernel(
    flags, q_ref, k_ref, v_ref, out_ref,
    kbuf, vbuf, peak, total, numer, bias, done,
    y_send, y_recv, z_send, z_recv, x_send, x_recv,
):
    ctx = lax.axis_index("ctx")
    kv = lax.axis_index("kv")
    z = ctx // NY
    y = ctx % NY

    def plane(d):
        return (z + d + NZ) % NZ

    def beside_y(d):
        return (y + d + NY) % NY

    def y_device(d):
        return {"ctx": z * NY + beside_y(d), "kv": kv}

    def z_device(d):
        return {"ctx": plane(d) * NY + y, "kv": kv}

    def x_device(j):
        return {"ctx": ctx, "kv": (kv + j) % NKV}

    barrier = pltpu.get_barrier_semaphore()
    for peer in [y_device(1), y_device(-1), z_device(1), z_device(-1)] + [x_device(j) for j in range(1, NKV)]:
        pl.semaphore_signal(barrier, inc=1, device_id=peer, device_id_type=MESH)

    mine = pl.ds(pl.multiple_of(ctx * BLOCK, BLOCK), BLOCK)
    kbuf[mine, :] = k_ref[...]
    vbuf[mine, :] = v_ref[...]
    pl.semaphore_wait(barrier, 4 + NKV - 1)

    bufs = {"k": kbuf, "v": vbuf}
    started = {}
    y_numbers, z_numbers = {}, {}

    def copy_rows(buf, start, size, peer, sems, number):
        rows = pl.ds(pl.multiple_of(start, HALF), size)
        return pltpu.make_async_remote_copy(
            src_ref=buf.at[rows, :],
            dst_ref=buf.at[rows, :],
            send_sem=sems[0].at[number],
            recv_sem=sems[1].at[number],
            device_id=peer,
            device_id_type=MESH,
        )

    def y_copy(name, d, hop, sign, receive):
        number = y_numbers.setdefault((name, d, hop, sign), len(y_numbers))
        back = hop if receive else hop - 1
        start = (plane(d) * NY + beside_y(-sign * back)) * BLOCK
        size = BLOCK
        if hop == 2:
            size = HALF
            start = start + (0 if sign > 0 else HALF)
        return copy_rows(bufs[name], start, size, y_device(sign), (y_send, y_recv), number)

    def z_copy(name, hop, sign, receive):
        number = z_numbers.setdefault((name, hop, sign), len(z_numbers))
        back = hop if receive else hop - 1
        p = plane(-sign * back)
        if name == "k":
            start, size = (p * NY + y) * BLOCK, BLOCK
        else:
            start, size = p * PLANE, PLANE
        if hop == 4:
            size = size // 2
            start = start + (0 if sign > 0 else size)
        return copy_rows(bufs[name], start, size, z_device(sign), (z_send, z_recv), number)

    def go(maker, *key):
        for sign in (1, -1):
            maker(*key, sign, False).start()
            started[(maker, *key, sign, False)] = None

    def arrive(maker, *key):
        for sign in (1, -1):
            maker(*key, sign, True).wait_recv()

    go(y_copy, "v", 0, 1)
    go(z_copy, "k", 1)
    go(y_copy, "k", 0, 1)

    peak[...] = jnp.full_like(peak, NEG)
    total[...] = jnp.zeros_like(total)
    numer[...] = jnp.zeros_like(numer)

    def compute(p, masked, between=None):
        rows = pl.ds(pl.multiple_of(p * PLANE, PLANE), PLANE)
        scores, weights, fades = {}, {}, {}
        far = p < z - WINDOW // PLANE

        def score(h):
            scores[h] = lax.dot_general(
                q_ref[:, h * HD:(h + 1) * HD], kbuf[rows, :],
                (((1,), (1,)), ((), ())), preferred_element_type=jnp.float32,
            )

        def weigh(h):
            s = scores.pop(h)
            old = peak[h]
            if masked:
                s = s + bias[flags[h]]
                new = jnp.maximum(old, jnp.max(s, axis=1, keepdims=True))
                low = new * SCALE
            else:
                shut = jnp.where(far, (1 - flags[h]).astype(jnp.float32) * NEG, 0.0)
                new = jnp.maximum(old, jnp.max(s, axis=1, keepdims=True) + shut)
                low = new * SCALE - shut
            weights[h] = jnp.exp2(s * SCALE - jnp.tile(low, (1, PLANE // HD))).astype(jnp.bfloat16)
            fades[h] = jnp.exp2((old - new) * SCALE)
            peak[h] = new

        def add(h):
            piece = vbuf[rows, :]
            piece = jnp.concatenate([piece, jnp.ones_like(piece)], axis=1)
            sums = jnp.dot(weights.pop(h), piece, preferred_element_type=jnp.float32)
            fade = fades.pop(h)
            total[h] = total[h] * fade + sums[:, HD:]
            numer[h] = numer[h] * fade + sums[:, :HD]

        score(0)
        for h in range(HQ):
            if h + 1 < HQ:
                score(h + 1)
            weigh(h)
            if h > 0:
                add(h - 1)
            if between is not None and h == HQ // 2 - 1:
                between()
        add(HQ - 1)

    def make_bias(p):
        def some(i, _):
            rows = pl.ds(pl.multiple_of(i * 32, 32), 32)
            t = ctx * BLOCK + i * 32 + lax.broadcasted_iota(jnp.int32, (32, PLANE), 0)
            s = p * PLANE + lax.broadcasted_iota(jnp.int32, (32, PLANE), 1)
            causal = s <= t
            near = (s < SINK) | (t - s < WINDOW)
            bias[1, rows, :] = jnp.where(causal, 0.0, NEG)
            bias[0, rows, :] = jnp.where(causal & near, 0.0, NEG)
            return 0

        lax.fori_loop(0, BLOCK // 32, some, 0)

    arrive(y_copy, "v", 0, 1)
    go(y_copy, "v", 0, 2)
    arrive(z_copy, "k", 1)
    go(z_copy, "k", 2)
    arrive(y_copy, "k", 0, 1)
    go(y_copy, "k", 0, 2)
    go(y_copy, "k", 1, 1)
    go(y_copy, "k", -1, 1)
    arrive(y_copy, "v", 0, 2)
    go(z_copy, "v", 1)
    arrive(y_copy, "k", 0, 2)

    def step(i):
        if i == 1:
            arrive(y_copy, "k", 1, 1)
            go(y_copy, "k", 1, 2)
            arrive(y_copy, "k", -1, 1)
            go(y_copy, "k", -1, 2)
            arrive(z_copy, "k", 2)
            go(z_copy, "k", 3)
            go(y_copy, "k", 2, 1)
            go(y_copy, "k", -2, 1)
            arrive(z_copy, "v", 1)
            go(z_copy, "v", 2)
            arrive(y_copy, "k", 1, 2)
            arrive(y_copy, "k", -1, 2)
        elif i == 2:
            arrive(y_copy, "k", 2, 1)
            go(y_copy, "k", 2, 2)
            arrive(y_copy, "k", -2, 1)
            go(y_copy, "k", -2, 2)
            arrive(z_copy, "k", 3)
            go(z_copy, "k", 4)
            go(y_copy, "k", 3, 1)
            go(y_copy, "k", -3, 1)
        elif i == 3:
            arrive(z_copy, "v", 2)
            go(z_copy, "v", 3)
            arrive(y_copy, "k", 2, 2)
            arrive(y_copy, "k", -2, 2)
        elif i == 4:
            arrive(y_copy, "k", 3, 1)
            go(y_copy, "k", 3, 2)
            arrive(y_copy, "k", -3, 1)
            go(y_copy, "k", -3, 2)
            arrive(z_copy, "k", 4)
            go(y_copy, "k", 4, 1)
        elif i == 5:
            arrive(z_copy, "v", 3)
            go(z_copy, "v", 4)
            arrive(y_copy, "k", 3, 2)
            arrive(y_copy, "k", -3, 2)
        elif i == 6:
            arrive(y_copy, "k", 4, 1)
            go(y_copy, "k", 4, 2)
        elif i == 7:
            arrive(z_copy, "v", 4)
            arrive(y_copy, "k", 4, 2)

    def one(i, _):
        for k in range(1, NZ):
            pl.when(i == k)(functools.partial(step, k))
        ring = (i + 1) // 2
        p = (z + jnp.where(i % 2 == 0, ring, -ring) + NZ) % NZ
        edge = z - WINDOW // PLANE
        masked = (p == z) | (p == edge) | ((p == 0) & (edge > 0))

        @pl.when((p <= z) & masked)
        def _():
            make_bias(p)
            compute(p, True)

        @pl.when((p <= z) & jnp.logical_not(masked))
        def _():
            compute(p, False)

        return 0

    lax.fori_loop(0, NZ, one, 0)

    def x_copy(j, g, receive):
        number = (j - 1) * GROUPS + g
        rows = (kv + j) % NKV * (BLOCK // NKV)
        columns = ((kv - j + NKV) % NKV if receive else kv) * (HQ * HD) + g * WIDE
        return pltpu.make_async_remote_copy(
            src_ref=done.at[pl.ds(pl.multiple_of(rows, BLOCK // NKV), BLOCK // NKV), pl.ds(g * WIDE, WIDE)],
            dst_ref=out_ref.at[:, pl.ds(pl.multiple_of(columns, WIDE), WIDE)],
            send_sem=x_send.at[number],
            recv_sem=x_recv.at[number],
            device_id=x_device(j),
            device_id_type=MESH,
        )

    for g in range(GROUPS):
        for h in range(g * HQ // GROUPS, (g + 1) * HQ // GROUPS):
            done[:, h * HD:(h + 1) * HD] = (numer[h] / total[h]).astype(jnp.bfloat16)
        for j in range(1, NKV):
            x_copy(j, g, False).start()
            started[(x_copy, j, g, False)] = None
    own = pl.ds(pl.multiple_of(kv * (BLOCK // NKV), BLOCK // NKV), BLOCK // NKV)
    out_ref[:, pl.ds(pl.multiple_of(kv * (HQ * HD), HQ * HD), HQ * HD)] = done[own, :]
    for g in range(GROUPS):
        for j in range(1, NKV):
            x_copy(j, g, True).wait_recv()
    for maker, *key in started:
        maker(*key).wait_send()


def shards(queries, keys, values, retrieval):
    rows = queries.shape[0]
    vmem = pl.BlockSpec(memory_space=pltpu.VMEM)
    state = pltpu.VMEM((HQ, rows, HD), jnp.float32)
    n_y = 2 * 2 * (1 + NZ)
    n_z = 2 * 2 * 4
    n_x = (NKV - 1) * GROUPS
    return pl.pallas_call(
        kernel,
        out_shape=jax.ShapeDtypeStruct((rows // NKV, NKV * HQ * HD), jnp.bfloat16),
        in_specs=[pl.BlockSpec(memory_space=pltpu.SMEM), vmem, vmem, vmem],
        out_specs=vmem,
        scratch_shapes=[
            pltpu.VMEM((NZ * PLANE, HD), jnp.bfloat16),
            pltpu.VMEM((NZ * PLANE, HD), jnp.bfloat16),
            state, state, state,
            pltpu.VMEM((2, rows, PLANE), jnp.float32),
            pltpu.VMEM((rows, HQ * HD), jnp.bfloat16),
            pltpu.SemaphoreType.DMA((n_y,)),
            pltpu.SemaphoreType.DMA((n_y,)),
            pltpu.SemaphoreType.DMA((n_z,)),
            pltpu.SemaphoreType.DMA((n_z,)),
            pltpu.SemaphoreType.DMA((n_x,)),
            pltpu.SemaphoreType.DMA((n_x,)),
        ],
        compiler_params=pltpu.CompilerParams(
            collective_id=0, has_side_effects=True, vmem_limit_bytes=48 * 1024 * 1024
        ),
    )(retrieval, queries, keys, values)


def solution(mesh):
    return jax.shard_map(
        shards,
        mesh=mesh,
        in_specs=(P("ctx", "kv"), P("ctx", "kv"), P("ctx", "kv"), P("kv")),
        out_specs=P(("ctx", "kv"), None),
        check_vma=False,
    )
```

time: 439 us -> 56.8 us (0.13); the launches traced: 433 us -> 56.4 us
  waiting for transfers between devices: 149 us -> 0 us
  other arithmetic: 122 us -> 0 us
  local copies, waits for them, and re-layouts: 77.4 us -> 4.17 us
  Pallas kernels: 0 us -> 52.2 us
  matrix products: 34 us -> 0 us
  loops' own time: 19.7 us -> 0 us
  blocking collectives: 17.9 us -> 0 us
  between operations: 13.5 us -> 0.01 us
    all_gather x2 -> x0, waiting for transfers between devices: 148 us -> none  [the longest x1 77.8 us: shards(): lax.all_gather(values, 'ctx', axis=0, tiled=True)]
    and x8 -> x0, other arithmetic: 100 us -> none  [compute(): allowed = causal & ((flag == 1) | near)]
    le x16 -> x0, local copies, waits for them, and re-layouts: 63.9 us -> none  [attend(): causal = spos[None, :] <= tpos[:, None]]
    pallas_call x0 -> x1, Pallas kernels: none -> 52.2 us  [shards(): pl.pallas_call(kernel, out_shape=jax.ShapeDtypeStruct((rows // NKV, NKV *...]
    dot_general x16 -> x0, matrix products: 34 us -> none  [the longest x8 17.2 us: compute(): jnp.dot(weights.astype(jnp.bfloat16), v_piece, preferred_element_type=jnp...]
    another operation x9 -> x0, loops' own time: 19.7 us -> none  [the longest x1 14.7 us: attend(): return lax.map(one_head, (peak, total, numer, q_heads, flags))]
    all_to_all x1 -> x0, blocking collectives: 17.9 us -> none  [shards(): lax.all_to_all(attention, 'kv', split_axis=0, concat_axis=1, tiled=True)]
    reduce_sum x8 -> x0, other arithmetic: 16.5 us -> none  [compute(): new_total = total * fade + jnp.sum(weights, axis=1)]
  transfers between devices with their start and end apart: 2 -> 0, of which waited for: 2 -> 0; matrix products, arithmetic and copies ran while one was open for 1% -> 0% of each run, Pallas kernels for 0% -> 0%
where the time goes in v1:
time: 56.8 us; the launch traced here: 56.4 us
  Pallas kernels  52.2 us (92%)
  local copies, waits for them, and re-layouts  4.17 us (7%)
    pallas_call x1, Pallas kernels, shards(): pl.pallas_call(kernel, out_shape=jax.ShapeDtypeStruct((rows // NKV, NKV *...  52.2 us
    unnamed x9, local copies, waits for them, and re-layouts  4.17 us

profile of v1, /device:TPU:225, one launch (start us, length us, event | category | flops | bytes accessed | tf_op | source)
XLA Modules:
  0.0 56.4 jit_solution(1764659494624621700)
XLA Ops:
  0.0 0.0 copy-start
  0.0 1.0 %copy-done = bf16[256,1024]{1,0:T(8,128)(2,1)S(1)} copy-done((bf16[256,1024]{1,0:T(8,128)(2,1)S(1)}, bf16[256,1024]{1,0:T(8,128)(2,1)}, u32[]{:S(2)}) %copy-start) | copy-done | bytes 524312
  1.0 0.0 copy-start.1
  1.0 0.8 %copy-done.1 = bf16[256,128]{1,0:T(8,128)(2,1)S(1)} copy-done((bf16[256,128]{1,0:T(8,128)(2,1)S(1)}, bf16[256,128]{1,0:T(8,128)(2,1)}, u32[]{:S(2)}) %copy-start.1) | copy-done | bytes 65560
  1.9 0.0 copy-start.2
  1.9 0.8 %copy-done.2 = bf16[256,128]{1,0:T(8,128)(2,1)S(1)} copy-done((bf16[256,128]{1,0:T(8,128)(2,1)S(1)}, bf16[256,128]{1,0:T(8,128)(2,1)}, u32[]{:S(2)}) %copy-start.2) | copy-done | bytes 65560
  2.7 0.0 copy-start.3
  2.7 0.7 %copy-done.3 = s32[8]{0:T(128)S(1)} copy-done((s32[8]{0:T(128)S(1)}, s32[8]{0:T(128)}, u32[]{:S(2)}) %copy-start.3) | copy-done | bytes 56
  3.4 52.2 %shard_map.46 = bf16[32,8192]{1,0:T(8,128)(2,1)S(1)} custom-call(s32[8]{0:T(128)S(1)} %copy-done.3, bf16[256,1024]{1,0:T(8,128)(2,1)S(1)} %copy-done, bf16[256,128]{1,0:T(8,128)(2,1)S(1)} %copy-done.1, bf16[256,128]{1,0:T(8,128)(2,1)S(1)} %copy-done.2), custom_call_target="tpu_custom_call" | custom-call | tf_op jit(solution)/shard_map/pallas_call | solution.py:290
  55.6 0.8 %copy.6 = bf16[32,8192]{1,0:T(8,128)(2,1)} copy(bf16[32,8192]{1,0:T(8,128)(2,1)S(1)} %shard_map.46) | data formatting | bytes 1048576
Async XLA Ops:
  0.0 1.0 %copy-start = (bf16[256,1024]{1,0:T(8,128)(2,1)S(1)}, bf16[256,1024]{1,0:T(8,128)(2,1)}, u32[]{:S(2)}) copy-start(bf16[256,1024]{1,0:T(8,128)(2,1)} %q_ref.1) | copy-start | bytes 1572868
  1.0 0.8 %copy-start.1 = (bf16[256,128]{1,0:T(8,128)(2,1)S(1)}, bf16[256,128]{1,0:T(8,128)(2,1)}, u32[]{:S(2)}) copy-start(bf16[256,128]{1,0:T(8,128)(2,1)} %k_ref.1) | copy-start | bytes 196612
  1.9 0.8 %copy-start.2 = (bf16[256,128]{1,0:T(8,128)(2,1)S(1)}, bf16[256,128]{1,0:T(8,128)(2,1)}, u32[]{:S(2)}) copy-start(bf16[256,128]{1,0:T(8,128)(2,1)} %v_ref.1) | copy-start | bytes 196612
  2.7 0.7 %copy-start.3 = (s32[8]{0:T(128)S(1)}, s32[8]{0:T(128)}, u32[]{:S(2)}) copy-start(s32[8]{0:T(128)} %flags.1) | copy-start | bytes 100

commit v2 on v1

v2 whole, which is shorter than its diff:
```python
import functools

import jax
import jax.numpy as jnp
from jax import lax
from jax.experimental import pallas as pl
from jax.experimental.pallas import tpu as pltpu
from jax.sharding import PartitionSpec as P

HD = 128
HQ = 8
SINK = 64
WINDOW = 4096
NEG = -1e30
SCALE = HD ** (-0.5) * 1.4426950408889634

NY = 4
NZ = 8
NKV = 8
PARTS = {"k": 2, "v": NY}
BLOCK = 256
PLANE = NY * BLOCK
HALF = BLOCK // 2
GROUPS = 4
WIDE = HQ * HD // GROUPS
MESH = pl.DeviceIdType.MESH


def kernel(
    flags_hbm, q_hbm, k_hbm, v_hbm, out_ref,
    flags, q_ref, kbuf, vbuf, peak, total, numer, bias, done,
    local_sem, y_send, y_recv, z_send, z_recv, x_send, x_recv,
):
    ctx = lax.axis_index("ctx")
    kv = lax.axis_index("kv")
    z = ctx // NY
    y = ctx % NY

    def plane(d):
        return (z + d + NZ) % NZ

    def beside(d):
        return (y + d + NY) % NY

    def y_device(d):
        return {"ctx": z * NY + beside(d), "kv": kv}

    def z_device(d):
        return {"ctx": plane(d) * NY + y, "kv": kv}

    def x_device(j):
        return {"ctx": ctx, "kv": (kv + j) % NKV}

    barrier = pltpu.get_barrier_semaphore()

    def greet(peer):
        pl.semaphore_signal(barrier, inc=1, device_id=peer, device_id_type=MESH)

    for d in range(1, NY):
        greet(y_device(d))
    for j in range(1, NKV):
        greet(x_device(j))
    pl.when(z > 0)(functools.partial(greet, z_device(-1)))
    pl.when((z != NZ // 2 - 1))(functools.partial(greet, z_device(1)))
    expected = NY - 1 + NKV - 1 + jnp.where(z < NZ - 1, 1, 0) + jnp.where(z != NZ // 2, 1, 0)

    def rows_of(start, size):
        return pl.ds(pl.multiple_of(start, HALF), size)

    mine = rows_of(ctx * BLOCK, BLOCK)
    local = [
        pltpu.make_async_copy(v_hbm, vbuf.at[mine, :], local_sem.at[0]),
        pltpu.make_async_copy(k_hbm, kbuf.at[mine, :], local_sem.at[1]),
        pltpu.make_async_copy(flags_hbm, flags, local_sem.at[2]),
        pltpu.make_async_copy(q_hbm, q_ref, local_sem.at[3]),
    ]
    for copy in local:
        copy.start()
    pl.semaphore_wait(barrier, expected)

    bufs = {"k": kbuf, "v": vbuf}
    started = {}
    numbers = {}

    def remote(src, dst, peer, sems, key):
        count = len([k for k in numbers if k[0] == key[0]])
        number = numbers.setdefault(key, count)
        return pltpu.make_async_remote_copy(
            src_ref=src,
            dst_ref=dst,
            send_sem=sems[0].at[number],
            recv_sem=sems[1].at[number],
            device_id=peer,
            device_id_type=MESH,
        )

    def y_copy(name, d, way, receive):
        rows = rows_of((plane(d) * NY + (beside(-way) if receive else y)) * BLOCK, BLOCK)
        dst = bufs[name].at[rows, :]
        src = {"k": k_hbm, "v": v_hbm}[name] if d == 0 else dst
        return remote(src, dst, y_device(way), (y_send, y_recv), ("y", name, d, way))

    def z_copy(name, hop, sign, part, receive):
        p = plane(-sign * (hop if receive else hop - 1))
        if name == "k":
            rows = rows_of((p * NY + y) * BLOCK + part * HALF, HALF)
        else:
            rows = rows_of((p * NY + beside(part)) * BLOCK, BLOCK)
        ref = bufs[name].at[rows, :]
        src = ref
        if hop == 1 and not receive:
            if name == "k":
                src = k_hbm.at[pl.ds(part * HALF, HALF), :]
            elif part == 0:
                src = v_hbm
        return remote(src, ref, z_device(sign), (z_send, z_recv), ("z", name, hop, sign, part))

    def last_hop(name, sign, part):
        return NZ // 2 if (part < PARTS[name] // 2) == (sign > 0) else NZ // 2 - 1

    def needed(name, hop, sign, part, receive):
        if sign > 0:
            return z >= hop if receive else (z >= hop - 1) & (z < NZ - 1)
        return plane(hop if receive else hop - 1) < last_hop(name, sign, part)

    def go(maker, *key, when=None):
        def start():
            maker(*key, False).start()

        def end():
            maker(*key, False).wait_send()

        if when is None:
            start()
        else:
            pl.when(when())(start)
        started[(maker, *key)] = (end, when)

    def arrive(maker, *key, when=None):
        def wait():
            maker(*key, True).wait_recv()

        if when is None:
            wait()
        else:
            pl.when(when())(wait)

    def go_y(name, back):
        for way in (1, -1, 2):
            go(y_copy, name, -back, way, when=lambda: z >= back)

    def arrive_y(name, back):
        for way in (1, -1, 2):
            arrive(y_copy, name, -back, way, when=lambda: z >= back)

    def send_on(name, hop, sign, part):
        if hop <= last_hop(name, sign, part):
            go(z_copy, name, hop, sign, part, when=functools.partial(needed, name, hop, sign, part, False))

    def pass_on(name, hop):
        for part in range(PARTS[name]):
            for sign in (1, -1):
                if hop <= last_hop(name, sign, part):
                    arrive(z_copy, name, hop, sign, part, when=functools.partial(needed, name, hop, sign, part, True))
                    send_on(name, hop + 1, sign, part)

    go_y("v", 0)
    for sign in (1, -1):
        for part in range(PARTS["k"]):
            send_on("k", 1, sign, part)
        send_on("v", 1, sign, 0)
    go_y("k", 0)

    peak[...] = jnp.full_like(peak, NEG)
    total[...] = jnp.zeros_like(total)
    numer[...] = jnp.zeros_like(numer)

    def compute(p, masked, after=None):
        rows = pl.ds(pl.multiple_of(p * PLANE, PLANE), PLANE)
        scores, weights, fades = {}, {}, {}
        far = p < z - WINDOW // PLANE

        def score(h):
            scores[h] = lax.dot_general(
                q_ref[:, h * HD:(h + 1) * HD], kbuf[rows, :],
                (((1,), (1,)), ((), ())), preferred_element_type=jnp.float32,
            )

        def weigh(h):
            s = scores.pop(h)
            old = peak[h]
            if masked:
                s = s + bias[flags[h]]
                new = jnp.maximum(old, jnp.max(s, axis=1, keepdims=True))
                low = new * SCALE
            else:
                shut = jnp.where(far, (1 - flags[h]).astype(jnp.float32) * NEG, 0.0)
                new = jnp.maximum(old, jnp.max(s, axis=1, keepdims=True) + shut)
                low = new * SCALE - shut
            weights[h] = jnp.exp2(s * SCALE - jnp.tile(low, (1, PLANE // HD))).astype(jnp.bfloat16)
            fades[h] = jnp.exp2((old - new) * SCALE)
            peak[h] = new

        def add(h):
            piece = vbuf[rows, :]
            piece = jnp.concatenate([piece, jnp.ones_like(piece)], axis=1)
            sums = jnp.dot(weights.pop(h), piece, preferred_element_type=jnp.float32)
            fade = fades.pop(h)
            total[h] = total[h] * fade + sums[:, HD:]
            numer[h] = numer[h] * fade + sums[:, :HD]

        score(0)
        for h in range(HQ):
            if h + 1 < HQ:
                score(h + 1)
            weigh(h)
            if h > 0:
                add(h - 1)
                if after is not None:
                    after(h - 1)
        add(HQ - 1)
        if after is not None:
            after(HQ - 1)

    def make_bias(p):
        def some(i, _):
            rows = pl.ds(pl.multiple_of(i * 32, 32), 32)
            t = ctx * BLOCK + i * 32 + lax.broadcasted_iota(jnp.int32, (32, PLANE), 0)
            s = p * PLANE + lax.broadcasted_iota(jnp.int32, (32, PLANE), 1)
            causal = s <= t
            near = (s < SINK) | (t - s < WINDOW)
            bias[1, rows, :] = jnp.where(causal, 0.0, NEG)
            bias[0, rows, :] = jnp.where(causal & near, 0.0, NEG)
            return 0

        lax.fori_loop(0, BLOCK // 32, some, 0)

    make_bias(z)
    for copy in local:
        copy.wait()
    pass_on("k", 1)
    go_y("k", 1)
    arrive_y("v", 0)
    for part in range(1, PARTS["v"]):
        for sign in (1, -1):
            send_on("v", 1, sign, part)
    arrive_y("k", 0)
    go_y("k", 7)
    compute(z, True)

    def step(i):
        if i == 1:
            pass_on("k", 2)
            go_y("k", 2)
            go_y("k", 6)
            pass_on("v", 1)
            arrive_y("k", 1)
        elif i == 2:
            pass_on("k", 3)
            go_y("k", 3)
            go_y("k", 5)
            arrive_y("k", 7)
        elif i == 3:
            pass_on("v", 2)
            pass_on("k", 4)
            go_y("k", 4)
            arrive_y("k", 2)
        elif i == 4:
            arrive_y("k", 6)
        elif i == 5:
            pass_on("v", 3)
            arrive_y("k", 3)
        elif i == 6:
            arrive_y("k", 5)

    edge = z - WINDOW // PLANE

    def one(i, _):
        for k in range(1, NZ - 1):
            pl.when(i == k)(functools.partial(step, k))
        ring = (i + 1) // 2
        p = (z + jnp.where(i % 2 == 0, ring, -ring) + NZ) % NZ
        masked = (p == 0) & (edge > 0)

        @pl.when((p < z) & masked)
        def _():
            make_bias(p)
            compute(p, True)

        @pl.when((p < z) & jnp.logical_not(masked))
        def _():
            compute(p, False)

        return 0

    lax.fori_loop(1, NZ - 1, one, 0)

    def x_copy(j, g, receive):
        rows = (kv + j) % NKV * (BLOCK // NKV)
        columns = ((kv - j + NKV) % NKV if receive else kv) * (HQ * HD) + g * WIDE
        return remote(
            done.at[pl.ds(pl.multiple_of(rows, BLOCK // NKV), BLOCK // NKV), pl.ds(g * WIDE, WIDE)],
            out_ref.at[:, pl.ds(pl.multiple_of(columns, WIDE), WIDE)],
            x_device(j), (x_send, x_recv), ("x", j, g),
        )

    def finish(h):
        done[:, h * HD:(h + 1) * HD] = (numer[h] / total[h]).astype(jnp.bfloat16)
        if (h + 1) % (HQ // GROUPS) == 0:
            for j in range(1, NKV):
                go(x_copy, j, h // (HQ // GROUPS))

    pass_on("v", NZ // 2)
    arrive_y("k", 4)

    @pl.when(edge >= 0)
    def _():
        make_bias(edge)
        compute(edge, True, finish)

    @pl.when(edge < 0)
    def _():
        for h in range(HQ):
            finish(h)

    own = pl.ds(pl.multiple_of(kv * (BLOCK // NKV), BLOCK // NKV), BLOCK // NKV)
    out_ref[:, pl.ds(pl.multiple_of(kv * (HQ * HD), HQ * HD), HQ * HD)] = done[own, :]
    for g in range(GROUPS):
        for j in range(1, NKV):
            arrive(x_copy, j, g)
    for end, when in started.values():
        if when is None:
            end()
        else:
            pl.when(when())(end)


def shards(queries, keys, values, retrieval):
    rows = queries.shape[0]
    state = pltpu.VMEM((HQ, rows, HD), jnp.float32)
    n_y = (NY - 1) * (1 + NZ)
    n_z = (PARTS["k"] + PARTS["v"]) * 7
    n_x = (NKV - 1) * GROUPS
    return pl.pallas_call(
        kernel,
        out_shape=jax.ShapeDtypeStruct((rows // NKV, NKV * HQ * HD), jnp.bfloat16),
        in_specs=[pl.BlockSpec(memory_space=pltpu.HBM)] * 4,
        out_specs=pl.BlockSpec(memory_space=pltpu.VMEM),
        scratch_shapes=[
            pltpu.SMEM((HQ,), jnp.int32),
            pltpu.VMEM((rows, HQ * HD), jnp.bfloat16),
            pltpu.VMEM((NZ * PLANE, HD), jnp.bfloat16),
            pltpu.VMEM((NZ * PLANE, HD), jnp.bfloat16),
            state, state, state,
            pltpu.VMEM((2, rows, PLANE), jnp.float32),
            pltpu.VMEM((rows, HQ * HD), jnp.bfloat16),
            pltpu.SemaphoreType.DMA((4,)),
            pltpu.SemaphoreType.DMA((n_y,)),
            pltpu.SemaphoreType.DMA((n_y,)),
            pltpu.SemaphoreType.DMA((n_z,)),
            pltpu.SemaphoreType.DMA((n_z,)),
            pltpu.SemaphoreType.DMA((n_x,)),
            pltpu.SemaphoreType.DMA((n_x,)),
        ],
        compiler_params=pltpu.CompilerParams(
            collective_id=0, has_side_effects=True, vmem_limit_bytes=62 * 1024 * 1024
        ),
    )(retrieval, queries, keys, values)


def solution(mesh):
    return jax.shard_map(
        shards,
        mesh=mesh,
        in_specs=(P("ctx", "kv"), P("ctx", "kv"), P("ctx", "kv"), P("kv")),
        out_specs=P(("ctx", "kv"), None),
        check_vma=False,
    )
```

time: 56.8 us -> 51.3 us (0.903)
  Pallas kernels: 52.2 us -> 48.7 us
  local copies, waits for them, and re-layouts: 4.17 us -> 1.87 us
    pallas_call x1, Pallas kernels: 52.2 us -> 48.7 us  [shards(): pl.pallas_call(kernel, out_shape=jax.ShapeDtypeStruct((rows // NKV, NKV *...]
    unnamed x9 -> x1, local copies, waits for them, and re-layouts: 4.17 us -> 1.87 us
where the time goes in v2:
time: 51.3 us; the launch traced here: 50.5 us
  Pallas kernels  48.7 us (95%)
  local copies, waits for them, and re-layouts  1.87 us (4%)
    pallas_call x1, Pallas kernels, shards(): pl.pallas_call(kernel, out_shape=jax.ShapeDtypeStruct((rows // NKV, NKV *...  48.7 us
    unnamed x1, local copies, waits for them, and re-layouts  1.87 us

profile of v2, /device:TPU:225, one launch (start us, length us, event | category | flops | bytes accessed | tf_op | source)
XLA Modules:
  0.0 50.5 jit_solution(12841392136494387593)
XLA Ops:
  0.0 48.7 %shard_map.46 = bf16[32,8192]{1,0:T(8,128)(2,1)} custom-call(s32[8]{0:T(128)} %flags_hbm.1, bf16[256,1024]{1,0:T(8,128)(2,1)} %q_hbm.1, bf16[256,128]{1,0:T(8,128)(2,1)} %k_hbm.1, bf16[256,128]{1,0:T(8,128)(2,1)} %v_hbm.1), custom_call_target="tpu_custom_call" | custom-call | tf_op jit(solution)/shard_map/pallas_call | solution.py:344
  48.7 1.9 %copy.6 = bf16[32,8192]{1,0:T(8,128)(2,1)} copy(bf16[32,8192]{1,0:T(8,128)(2,1)} %shard_map.46) | data formatting | bytes 1048576

commit v3 on v2

--- a/solution.py
+++ b/solution.py
@@ -28,7 +28,7 @@
 
 def kernel(
     flags_hbm, q_hbm, k_hbm, v_hbm, out_ref,
-    flags, q_ref, kbuf, vbuf, peak, total, numer, bias, done,
+    flags, q_ref, kbuf, vbuf, peak, total, numer, own_bias, edge_bias, done,
     local_sem, y_send, y_recv, z_send, z_recv, x_send, x_recv,
 ):
     ctx = lax.axis_index("ctx")
@@ -175,10 +175,9 @@
     total[...] = jnp.zeros_like(total)
     numer[...] = jnp.zeros_like(numer)
 
-    def compute(p, masked, after=None):
-        rows = pl.ds(pl.multiple_of(p * PLANE, PLANE), PLANE)
+    def compute(start, size, term, after=None):
+        rows = pl.ds(pl.multiple_of(start, BLOCK), size)
         scores, weights, fades = {}, {}, {}
-        far = p < z - WINDOW // PLANE
 
         def score(h):
             scores[h] = lax.dot_general(
@@ -187,17 +186,10 @@
             )
 
         def weigh(h):
-            s = scores.pop(h)
+            s = scores.pop(h) + term(h)
             old = peak[h]
-            if masked:
-                s = s + bias[flags[h]]
-                new = jnp.maximum(old, jnp.max(s, axis=1, keepdims=True))
-                low = new * SCALE
-            else:
-                shut = jnp.where(far, (1 - flags[h]).astype(jnp.float32) * NEG, 0.0)
-                new = jnp.maximum(old, jnp.max(s, axis=1, keepdims=True) + shut)
-                low = new * SCALE - shut
-            weights[h] = jnp.exp2(s * SCALE - jnp.tile(low, (1, PLANE // HD))).astype(jnp.bfloat16)
+            new = jnp.maximum(old, jnp.max(s, axis=1, keepdims=True))
+            weights[h] = jnp.exp2(s * SCALE - jnp.tile(new * SCALE, (1, size // HD))).astype(jnp.bfloat16)
             fades[h] = jnp.exp2((old - new) * SCALE)
             peak[h] = new
 
@@ -222,22 +214,43 @@
         if after is not None:
             after(HQ - 1)
 
-    def make_bias(p):
-        def some(i, _):
-            rows = pl.ds(pl.multiple_of(i * 32, 32), 32)
-            t = ctx * BLOCK + i * 32 + lax.broadcasted_iota(jnp.int32, (32, PLANE), 0)
-            s = p * PLANE + lax.broadcasted_iota(jnp.int32, (32, PLANE), 1)
-            causal = s <= t
-            near = (s < SINK) | (t - s < WINDOW)
-            bias[1, rows, :] = jnp.where(causal, 0.0, NEG)
-            bias[0, rows, :] = jnp.where(causal & near, 0.0, NEG)
-            return 0
-
-        lax.fori_loop(0, BLOCK // 32, some, 0)
-
-    make_bias(z)
+    edge = z - WINDOW // PLANE
+
+    def shut(h):
+        return (1 - flags[h]).astype(jnp.float32) * NEG
+
+    def block_of_own():
+        compute(ctx * BLOCK, BLOCK, lambda h: own_bias[...])
+
+    def blocks_before():
+        column = lax.broadcasted_iota(jnp.int32, (1, PLANE - BLOCK), 1)
+        row = jnp.where(column < y * BLOCK, 0.0, NEG)
+        compute(z * PLANE, PLANE - BLOCK, lambda h: row)
+
+    def whole_plane(p):
+        column = lax.broadcasted_iota(jnp.int32, (1, PLANE), 1)
+        row = jnp.where((p < edge) & (p * PLANE + column >= SINK), 1.0, 0.0)
+        compute(p * PLANE, PLANE, lambda h: row * shut(h))
+
+    def edge_plane(after):
+        compute(edge * PLANE, PLANE, lambda h: edge_bias[flags[h]], after)
+
+    own_bias[...] = jnp.where(
+        lax.broadcasted_iota(jnp.int32, (BLOCK, BLOCK), 1) <= lax.broadcasted_iota(jnp.int32, (BLOCK, BLOCK), 0), 0.0, NEG
+    )
     for copy in local:
         copy.wait()
+    block_of_own()
+
+    def some(i, _):
+        rows = pl.ds(pl.multiple_of(i * 32, 32), 32)
+        t = y * BLOCK + i * 32 + lax.broadcasted_iota(jnp.int32, (32, PLANE), 0)
+        s = lax.broadcasted_iota(jnp.int32, (32, PLANE), 1)
+        edge_bias[0, rows, :] = jnp.where((s > t) | (edge * PLANE + s < SINK), 0.0, NEG)
+        edge_bias[1, rows, :] = jnp.zeros((32, PLANE), jnp.float32)
+        return 0
+
+    lax.fori_loop(0, BLOCK // 32, some, 0)
     pass_on("k", 1)
     go_y("k", 1)
     arrive_y("v", 0)
@@ -246,7 +259,7 @@
             send_on("v", 1, sign, part)
     arrive_y("k", 0)
     go_y("k", 7)
-    compute(z, True)
+    pl.when(y > 0)(blocks_before)
 
     def step(i):
         if i == 1:
@@ -273,24 +286,12 @@
         elif i == 6:
             arrive_y("k", 5)
 
-    edge = z - WINDOW // PLANE
-
     def one(i, _):
         for k in range(1, NZ - 1):
             pl.when(i == k)(functools.partial(step, k))
         ring = (i + 1) // 2
         p = (z + jnp.where(i % 2 == 0, ring, -ring) + NZ) % NZ
-        masked = (p == 0) & (edge > 0)
-
-        @pl.when((p < z) & masked)
-        def _():
-            make_bias(p)
-            compute(p, True)
-
-        @pl.when((p < z) & jnp.logical_not(masked))
-        def _():
-            compute(p, False)
-
+        pl.when(p < z)(functools.partial(whole_plane, p))
         return 0
 
     lax.fori_loop(1, NZ - 1, one, 0)
@@ -315,8 +316,7 @@
 
     @pl.when(edge >= 0)
     def _():
-        make_bias(edge)
-        compute(edge, True, finish)
+        edge_plane(finish)
 
     @pl.when(edge < 0)
     def _():
@@ -352,6 +352,7 @@
             pltpu.VMEM((NZ * PLANE, HD), jnp.bfloat16),
             pltpu.VMEM((NZ * PLANE, HD), jnp.bfloat16),
             state, state, state,
+            pltpu.VMEM((rows, BLOCK), jnp.float32),
             pltpu.VMEM((2, rows, PLANE), jnp.float32),
             pltpu.VMEM((rows, HQ * HD), jnp.bfloat16),
             pltpu.SemaphoreType.DMA((4,)),

time: 51.3 us -> 49.9 us (0.973); the launches traced: 50.5 us -> 49.8 us
  Pallas kernels: 48.7 us -> 47.9 us
    pallas_call x1, Pallas kernels: 48.7 us -> 47.9 us  [shards(): pl.pallas_call(kernel, out_shape=jax.ShapeDtypeStruct((rows // NKV, NKV *...]
where the time goes in v3:
time: 49.9 us; the launch traced here: 49.8 us
  Pallas kernels  47.9 us (96%)
  local copies, waits for them, and re-layouts  1.87 us (4%)
    pallas_call x1, Pallas kernels, shards(): pl.pallas_call(kernel, out_shape=jax.ShapeDtypeStruct((rows // NKV, NKV *...  47.9 us
    unnamed x1, local copies, waits for them, and re-layouts  1.87 us

profile of v3, /device:TPU:225, one launch (start us, length us, event | category | flops | bytes accessed | tf_op | source)
XLA Modules:
  0.0 49.8 jit_solution(11537813891810947496)
XLA Ops:
  0.0 47.9 %shard_map.46 = bf16[32,8192]{1,0:T(8,128)(2,1)} custom-call(s32[8]{0:T(128)} %flags_hbm.1, bf16[256,1024]{1,0:T(8,128)(2,1)} %q_hbm.1, bf16[256,128]{1,0:T(8,128)(2,1)} %k_hbm.1, bf16[256,128]{1,0:T(8,128)(2,1)} %v_hbm.1), custom_call_target="tpu_custom_call" | custom-call | tf_op jit(solution)/shard_map/pallas_call | solution.py:344
  48.0 1.9 %copy.6 = bf16[32,8192]{1,0:T(8,128)(2,1)} copy(bf16[32,8192]{1,0:T(8,128)(2,1)} %shard_map.46) | data formatting | bytes 1048576

commit v4 on v3

--- a/solution.py
+++ b/solution.py
@@ -21,7 +21,7 @@
 BLOCK = 256
 PLANE = NY * BLOCK
 HALF = BLOCK // 2
-GROUPS = 4
+GROUPS = 2
 WIDE = HQ * HD // GROUPS
 MESH = pl.DeviceIdType.MESH
 
@@ -145,13 +145,19 @@
         else:
             pl.when(when())(wait)
 
+    def y_wanted(name, back, way, receive):
+        if back > 0:
+            return z >= back
+        later = beside(-way) < y if receive else beside(way) > y
+        return later if name == "k" else later | (z < NZ - 1)
+
     def go_y(name, back):
         for way in (1, -1, 2):
-            go(y_copy, name, -back, way, when=lambda: z >= back)
+            go(y_copy, name, -back, way, when=functools.partial(y_wanted, name, back, way, False))
 
     def arrive_y(name, back):
         for way in (1, -1, 2):
-            arrive(y_copy, name, -back, way, when=lambda: z >= back)
+            arrive(y_copy, name, -back, way, when=functools.partial(y_wanted, name, back, way, True))
 
     def send_on(name, hop, sign, part):
         if hop <= last_hop(name, sign, part):
@@ -169,7 +175,6 @@
         for part in range(PARTS["k"]):
             send_on("k", 1, sign, part)
         send_on("v", 1, sign, 0)
-    go_y("k", 0)
 
     peak[...] = jnp.full_like(peak, NEG)
     total[...] = jnp.zeros_like(total)
@@ -240,6 +245,7 @@
     )
     for copy in local:
         copy.wait()
+    go_y("k", 0)
     block_of_own()
 
     def some(i, _):
@@ -259,13 +265,13 @@
             send_on("v", 1, sign, part)
     arrive_y("k", 0)
     go_y("k", 7)
+    pass_on("k", 2)
+    go_y("k", 2)
+    go_y("k", 6)
     pl.when(y > 0)(blocks_before)
 
     def step(i):
         if i == 1:
-            pass_on("k", 2)
-            go_y("k", 2)
-            go_y("k", 6)
             pass_on("v", 1)
             arrive_y("k", 1)
         elif i == 2:
@@ -325,14 +331,20 @@
 
     own = pl.ds(pl.multiple_of(kv * (BLOCK // NKV), BLOCK // NKV), BLOCK // NKV)
     out_ref[:, pl.ds(pl.multiple_of(kv * (HQ * HD), HQ * HD), HQ * HD)] = done[own, :]
+    def finish_sends(last):
+        for (maker, *_), (end, when) in started.items():
+            if (maker is x_copy) != last:
+                continue
+            if when is None:
+                end()
+            else:
+                pl.when(when())(end)
+
+    finish_sends(False)
     for g in range(GROUPS):
         for j in range(1, NKV):
             arrive(x_copy, j, g)
-    for end, when in started.values():
-        if when is None:
-            end()
-        else:
-            pl.when(when())(end)
+    finish_sends(True)
 
 
 def shards(queries, keys, values, retrieval):

time: 49.9 us -> 49.6 us (level)
  no operation moved by 1% of the time
where the time goes in v4:
time: 49.6 us; the launch traced here: 49.3 us
  Pallas kernels  47.5 us (96%)
  local copies, waits for them, and re-layouts  1.87 us (4%)
    pallas_call x1, Pallas kernels, shards(): pl.pallas_call(kernel, out_shape=jax.ShapeDtypeStruct((rows // NKV, NKV *...  47.5 us
    unnamed x1, local copies, waits for them, and re-layouts  1.87 us

profile of v4, /device:TPU:225, one launch (start us, length us, event | category | flops | bytes accessed | tf_op | source)
XLA Modules:
  0.0 49.3 jit_solution(3923581352132183592)
XLA Ops:
  0.0 47.5 %shard_map.46 = bf16[32,8192]{1,0:T(8,128)(2,1)} custom-call(s32[8]{0:T(128)} %flags_hbm.1, bf16[256,1024]{1,0:T(8,128)(2,1)} %q_hbm.1, bf16[256,128]{1,0:T(8,128)(2,1)} %k_hbm.1, bf16[256,128]{1,0:T(8,128)(2,1)} %v_hbm.1), custom_call_target="tpu_custom_call" | custom-call | tf_op jit(solution)/shard_map/pallas_call | solution.py:356
  47.5 1.9 %copy.6 = bf16[32,8192]{1,0:T(8,128)(2,1)} copy(bf16[32,8192]{1,0:T(8,128)(2,1)} %shard_map.46) | data formatting | bytes 1048576

commit v5 on v4

--- a/solution.py
+++ b/solution.py
@@ -330,7 +330,10 @@
             finish(h)
 
     own = pl.ds(pl.multiple_of(kv * (BLOCK // NKV), BLOCK // NKV), BLOCK // NKV)
-    out_ref[:, pl.ds(pl.multiple_of(kv * (HQ * HD), HQ * HD), HQ * HD)] = done[own, :]
+    keep = pltpu.make_async_copy(
+        done.at[own, :], out_ref.at[:, pl.ds(pl.multiple_of(kv * (HQ * HD), HQ * HD), HQ * HD)], local_sem.at[4]
+    )
+    keep.start()
     def finish_sends(last):
         for (maker, *_), (end, when) in started.items():
             if (maker is x_copy) != last:
@@ -344,6 +347,7 @@
     for g in range(GROUPS):
         for j in range(1, NKV):
             arrive(x_copy, j, g)
+    keep.wait()
     finish_sends(True)
 
 
@@ -357,7 +361,7 @@
         kernel,
         out_shape=jax.ShapeDtypeStruct((rows // NKV, NKV * HQ * HD), jnp.bfloat16),
         in_specs=[pl.BlockSpec(memory_space=pltpu.HBM)] * 4,
-        out_specs=pl.BlockSpec(memory_space=pltpu.VMEM),
+        out_specs=pl.BlockSpec(memory_space=pltpu.HBM),
         scratch_shapes=[
             pltpu.SMEM((HQ,), jnp.int32),
             pltpu.VMEM((rows, HQ * HD), jnp.bfloat16),
@@ -367,7 +371,7 @@
             pltpu.VMEM((rows, BLOCK), jnp.float32),
             pltpu.VMEM((2, rows, PLANE), jnp.float32),
             pltpu.VMEM((rows, HQ * HD), jnp.bfloat16),
-            pltpu.SemaphoreType.DMA((4,)),
+            pltpu.SemaphoreType.DMA((5,)),
             pltpu.SemaphoreType.DMA((n_y,)),
             pltpu.SemaphoreType.DMA((n_y,)),
             pltpu.SemaphoreType.DMA((n_z,)),

time: 49.6 us -> 48.9 us (0.986)
  Pallas kernels: 47.5 us -> 46.8 us
    pallas_call x1, Pallas kernels: 47.5 us -> 46.8 us  [shards(): pl.pallas_call(kernel, out_shape=jax.ShapeDtypeStruct((rows // NKV, NKV *...]
where the time goes in v5:
time: 48.9 us; the launch traced here: 48.7 us
  Pallas kernels  46.8 us (96%)
  local copies, waits for them, and re-layouts  1.87 us (4%)
    pallas_call x1, Pallas kernels, shards(): pl.pallas_call(kernel, out_shape=jax.ShapeDtypeStruct((rows // NKV, NKV *...  46.8 us
    unnamed x1, local copies, waits for them, and re-layouts  1.87 us

profile of v5, /device:TPU:225, one launch (start us, length us, event | category | flops | bytes accessed | tf_op | source)
XLA Modules:
  0.0 48.7 jit_solution(10672579458316019342)
XLA Ops:
  0.0 46.8 %shard_map.46 = bf16[32,8192]{1,0:T(8,128)(2,1)} custom-call(s32[8]{0:T(128)} %flags_hbm.1, bf16[256,1024]{1,0:T(8,128)(2,1)} %q_hbm.1, bf16[256,128]{1,0:T(8,128)(2,1)} %k_hbm.1, bf16[256,128]{1,0:T(8,128)(2,1)} %v_hbm.1), custom_call_target="tpu_custom_call" | custom-call | tf_op jit(solution)/shard_map/pallas_call | solution.py:360
  46.8 1.9 %copy.6 = bf16[32,8192]{1,0:T(8,128)(2,1)} copy(bf16[32,8192]{1,0:T(8,128)(2,1)} %shard_map.46) | data formatting | bytes 1048576

commit v6 on v5

--- a/solution.py
+++ b/solution.py
@@ -180,7 +180,7 @@
     total[...] = jnp.zeros_like(total)
     numer[...] = jnp.zeros_like(numer)
 
-    def compute(start, size, term, after=None):
+    def compute(start, size, term, after=None, bar=None):
         rows = pl.ds(pl.multiple_of(start, BLOCK), size)
         scores, weights, fades = {}, {}, {}
 
@@ -191,10 +191,16 @@
             )
 
         def weigh(h):
-            s = scores.pop(h) + term(h)
+            s = scores.pop(h)
             old = peak[h]
-            new = jnp.maximum(old, jnp.max(s, axis=1, keepdims=True))
-            weights[h] = jnp.exp2(s * SCALE - jnp.tile(new * SCALE, (1, size // HD))).astype(jnp.bfloat16)
+            if bar is None:
+                s = s + term(h)
+                new = jnp.maximum(old, jnp.max(s, axis=1, keepdims=True))
+                low = new * SCALE
+            else:
+                new = jnp.maximum(old, jnp.max(s, axis=1, keepdims=True) + bar(h))
+                low = new * SCALE - bar(h)
+            weights[h] = jnp.exp2(s * SCALE - jnp.tile(low, (1, size // HD))).astype(jnp.bfloat16)
             fades[h] = jnp.exp2((old - new) * SCALE)
             peak[h] = new
 
@@ -235,7 +241,15 @@
     def whole_plane(p):
         column = lax.broadcasted_iota(jnp.int32, (1, PLANE), 1)
         row = jnp.where((p < edge) & (p * PLANE + column >= SINK), 1.0, 0.0)
-        compute(p * PLANE, PLANE, lambda h: row * shut(h))
+        sink = (p == 0) & (edge > 0)
+
+        @pl.when(sink)
+        def _():
+            compute(p * PLANE, PLANE, lambda h: row * shut(h))
+
+        @pl.when(jnp.logical_not(sink))
+        def _():
+            compute(p * PLANE, PLANE, None, bar=lambda h: jnp.where(p < edge, shut(h), 0.0))
 
     def edge_plane(after):
         compute(edge * PLANE, PLANE, lambda h: edge_bias[flags[h]], after)
@@ -314,7 +328,7 @@
     def finish(h):
         done[:, h * HD:(h + 1) * HD] = (numer[h] / total[h]).astype(jnp.bfloat16)
         if (h + 1) % (HQ // GROUPS) == 0:
-            for j in range(1, NKV):
+            for j in (4, 3, 5, 2, 6, 1, 7):
                 go(x_copy, j, h // (HQ // GROUPS))
 
     pass_on("v", NZ // 2)

time: 48.9 us -> 48.5 us (level)
  Pallas kernels: 46.8 us -> 46.2 us
    pallas_call x1, Pallas kernels: 46.8 us -> 46.2 us  [shards(): pl.pallas_call(kernel, out_shape=jax.ShapeDtypeStruct((rows // NKV, NKV *...]
where the time goes in v6:
time: 48.5 us; the launch traced here: 48.1 us
  Pallas kernels  46.2 us (95%)
  local copies, waits for them, and re-layouts  1.87 us (4%)
    pallas_call x1, Pallas kernels, shards(): pl.pallas_call(kernel, out_shape=jax.ShapeDtypeStruct((rows // NKV, NKV *...  46.2 us
    unnamed x1, local copies, waits for them, and re-layouts  1.87 us

profile of v6, /device:TPU:225, one launch (start us, length us, event | category | flops | bytes accessed | tf_op | source)
XLA Modules:
  0.0 48.1 jit_solution(3229846507089366879)
XLA Ops:
  0.0 46.2 %shard_map.46 = bf16[32,8192]{1,0:T(8,128)(2,1)} custom-call(s32[8]{0:T(128)} %flags_hbm.1, bf16[256,1024]{1,0:T(8,128)(2,1)} %q_hbm.1, bf16[256,128]{1,0:T(8,128)(2,1)} %k_hbm.1, bf16[256,128]{1,0:T(8,128)(2,1)} %v_hbm.1), custom_call_target="tpu_custom_call" | custom-call | tf_op jit(solution)/shard_map/pallas_call | solution.py:374
  46.2 1.9 %copy.6 = bf16[32,8192]{1,0:T(8,128)(2,1)} copy(bf16[32,8192]{1,0:T(8,128)(2,1)} %shard_map.46) | data formatting | bytes 1048576
